TPU v7x, 32 devices: a whole 2x2x4 slice. The times are simulated.
32 devices in a mesh: context: 8 (over z, x), channel: 4 (over y, core).
Axes of the slice: x: 2, y: 2, z: 4, core: 2. Of those that a mesh axis runs over, the one named last changes fastest.
Arguments:
- first_stream: bfloat16 [2048, 8192], P('context', 'channel'), may hold values from -6 to 6
- value_stream: bfloat16 [2048, 8192], P('context', 'channel'), may hold values from -6 to 6
- short_gate: bfloat16 [2048, 8192], P('context', 'channel'), may hold values from -6 to 6
- out_gate: bfloat16 [2048, 8192], P('context', 'channel'), may hold values from -250 to 250
- mr_filter: float32 [128, 8192], P(None, 'channel'), may hold values from -0.5 to 0.5
- li_residue: float32 [16, 8192], P(None, 'channel'), may hold values from -1.5 to 1.5
- li_rate: float32 [16, 8192], P(None, 'channel'), may hold values from 0.00014648438 to 0.05
- li_skip: float32 [8192], P('channel'), may hold values from 0.5 to 1.5
- norm_gain: float32 [8192], P('channel'), may hold values from 0.5 to 1.5
Outputs:
- mixed: bfloat16 [2048, 8192], P('context', 'channel')
All inputs are finite; a program needn't handle non-finite values.
Results may differ from a plain program's by a relative error of at most 0.0064.
Values may be sent and summed in bfloat16 or wider, within the bound.
A program may use at most 64 MiB of HBM per device.

v0:
```python
import functools

import jax
import jax.numpy as jnp
import numpy as np
from jax import lax
from jax.experimental import pallas as pl
from jax.experimental.pallas import tpu as pltpu
from jax.sharding import PartitionSpec as P

F32 = jnp.float32
BF16 = jnp.bfloat16
LANES = 128
SUB = 8


def split_const(a):
    hi = a.astype(BF16)
    lo = (a - hi.astype(np.float64)).astype(BF16)
    return hi, lo


def transforms(points, out_first, out_count, taps):
    freq = 2.0 * np.pi * (np.arange(points // 2) + 0.5) / points
    phase = freq[:, None] * np.arange(points)[None, :]
    full = np.concatenate([np.cos(phase), np.sin(phase)], 0)
    hi, lo = split_const(full[:, :taps])
    taps_m = np.concatenate([hi, hi, lo], 1)
    hi, lo = split_const(full)
    both = np.concatenate([hi, lo], 1)
    back = full[:, out_first : out_first + out_count].T * (2.0 / points)
    return both, taps_m, back.astype(BF16)


def dot(a, b):
    return lax.dot_general(a, b, (((1,), (0,)), ((), ())), preferred_element_type=F32)


def three(v):
    hi = v.astype(BF16)
    lo = (v - hi.astype(F32)).astype(BF16)
    return jnp.concatenate([hi, lo, hi], 0)


def times_spectrum(x, h):
    half = x.shape[0] // 2
    xc, xs, hc, hs = x[:half], x[half:], h[:half], h[half:]
    return jnp.concatenate([xc * hc - xs * hs, xc * hs + xs * hc], 0)


def sublane_index():
    return lax.broadcasted_iota(jnp.int32, (SUB, LANES), 0).astype(F32)


def mode_sums(start, step, blocks, put):
    for a in range(blocks):
        total = start[0]
        for v in start[1:]:
            total = total + v
        put(a, total)
        if a + 1 < blocks:
            start = [v * e for v, e in zip(start, step)]


def rows_of(ref, lanes):
    return [ref[r : r + 1, lanes] for r in range(ref.shape[0])]


MESH = pl.DeviceIdType.MESH


def fused_kernel(n_ctx, n_chan, chunk, *refs):
    n_in = 14
    (first_h, value_h, gate_h, og_h, filt_h, res_h, rate_h, skip_h, fs_h, gs_h, fsh_h, flh_h, fl_h, gl_h) = refs[:n_in]
    long_out, power_out = refs[n_in : n_in + 2]
    (first, value, gate, og, filt, res, rate, skip, fs, gs, fsh, flh, fl, gl) = refs[n_in + 2 : 2 * n_in + 2]
    (x, hs, hl, impulse, mixed, base, total, end, sent, got, state, power, pow_row, pow_got, amp, step8, fade) = refs[
        2 * n_in + 2 : 2 * n_in + 19
    ]
    in_sem, halo_send, halo_recv, st_send, st_recv, pow_send, pow_recv = refs[2 * n_in + 19 :]

    rows, width = first.shape
    taps = filt.shape[0]
    chunks = width // chunk
    here, lane_group = lax.axis_index("context"), lax.axis_index("channel")
    head, tail = pl.ds(0, rows - taps), pl.ds(rows - taps, taps)

    pairs = [
        (first_h.at[tail], first.at[tail]),
        (value_h.at[tail], value.at[tail]),
        (filt_h, filt),
        (fsh_h, fsh),
        (res_h, res),
        (rate_h, rate),
        (flh_h, flh),
        (first_h.at[head], first.at[head]),
        (value_h.at[head], value.at[head]),
        (fs_h, fs),
        (gs_h, gs),
        (gate_h, gate),
        (skip_h, skip),
        (fl_h, fl),
        (gl_h, gl),
        (og_h, og),
    ]
    loads = [pltpu.make_async_copy(a, b, in_sem.at[i]) for i, (a, b) in enumerate(pairs)]
    for load in loads:
        load.start()

    spans = []
    while 2 << len(spans) < n_ctx:
        spans.append(2 << len(spans))
    offsets = sorted({k % n_ctx for s in [1, 2] + spans for k in (s, -s)} - {0})
    barrier = pltpu.get_barrier_semaphore()
    for k in offsets:
        pl.semaphore_signal(barrier, inc=1, device_id={"context": lax.rem(here + k, n_ctx)}, device_id_type=MESH)
    for k in range(1, n_chan):
        pl.semaphore_signal(barrier, inc=1, device_id={"channel": lax.rem(lane_group + k, n_chan)}, device_id_type=MESH)
    loads[0].wait()
    loads[1].wait()
    pl.semaphore_wait(barrier, len(offsets) + n_chan - 1)

    def at_chunk(c):
        return pl.ds(pl.multiple_of(c * chunk, chunk), chunk)

    def product(part, cols):
        return (first[part, cols].astype(F32) * value[part, cols].astype(F32)).astype(BF16)

    def halo_copy(c):
        cols = at_chunk(c)
        return pltpu.make_async_remote_copy(
            src_ref=x.at[pl.ds(rows, taps), cols],
            dst_ref=x.at[pl.ds(0, taps), cols],
            send_sem=halo_send.at[c],
            recv_sem=halo_recv.at[c],
            device_id={"context": lax.rem(here + 1, n_ctx)},
            device_id_type=MESH,
        )

    @pl.loop(0, chunks)
    def _(c):
        cols = at_chunk(c)
        x[pl.ds(rows, taps), cols] = product(tail, cols)
        halo_copy(c).start()

    for load in loads[2:7]:
        load.wait()
    amp[...] = res[...] * jnp.sqrt(2.0 * rate[...])
    step8[...] = jnp.exp(-SUB * rate[...])

    sub = sublane_index()
    poles = rate.shape[0]
    half = chunks // 2

    def lane_tiles(c):
        return [pl.ds(pl.multiple_of(c * chunk + t, LANES), LANES) for t in range(0, chunk, LANES)]

    def steps(lanes):
        return [jnp.broadcast_to(step8[r : r + 1, lanes], (SUB, LANES)) for r in range(poles)]

    def present(k):
        return jnp.where(here >= k, 1.0, 0.0).astype(F32)

    def spectra(c):
        cols = at_chunk(c)
        for t, lanes in enumerate(lane_tiles(c)):
            start = []
            for r in range(poles):
                fading = jnp.exp(-rate[r : r + 1, lanes] * sub)
                fade[r, :, lanes] = fading
                start.append(amp[r : r + 1, lanes] * fading)

            def put(a, v):
                impulse[a * SUB : (a + 1) * SUB, t * LANES : (t + 1) * LANES] = v

            mode_sums(start, steps(lanes), rows // SUB, put)
        hs[:, cols] = dot(fsh[...], three(filt[:, cols]))
        hl[:, cols] = dot(flh[...], three(impulse[...]))

    def short(c):
        cols = at_chunk(c)
        halo_copy(c).wait_recv()
        before = (x[pl.ds(0, taps), cols].astype(F32) * present(1)).astype(BF16)
        window = jnp.concatenate([before, product(head, cols), x[pl.ds(rows, taps), cols]], 0)
        y = times_spectrum(dot(fs[...], jnp.concatenate([window, window], 0)), hs[:, cols])
        out = dot(gs[...], y.astype(BF16))
        mixed[:, cols] = (gate[:, cols].astype(F32) * out).astype(BF16)

    def ends(c):
        for lanes in lane_tiles(c):
            step = steps(lanes)
            sums = None
            for a in range(0, rows, 16):
                both = mixed[a : a + 16, lanes].astype(F32)
                for part in (both[:SUB], both[SUB:]):
                    sums = [part] * poles if sums is None else [s * e + part for s, e in zip(sums, step)]
            for r, s in enumerate(sums):
                fading = jnp.exp(-rate[r : r + 1, lanes] * (SUB - 1.0 - sub))
                end[r : r + 1, lanes] = jnp.sum(s * fading, axis=0, keepdims=True)

    def local_long(c):
        cols = at_chunk(c)
        here_x = mixed[:, cols]
        y = times_spectrum(dot(fl[...], jnp.concatenate([here_x, here_x], 0)), hl[:, cols])
        base[:, cols] = dot(gl[...], y.astype(BF16)) + skip[:, cols] * here_x.astype(F32)

    def carry(c):
        for lanes in lane_tiles(c):
            start = [state[r : r + 1, lanes] * fade[r, :, lanes] for r in range(poles)]

            def put(a, v):
                total[a * SUB : (a + 1) * SUB, :] = v

            mode_sums(start, steps(lanes), rows // SUB, put)
            out = (base[:, lanes] + total[...]).astype(BF16)
            long_out[:, lanes] = out
            gated = og[:, lanes].astype(F32) * out.astype(F32)
            power[...] += gated * gated

    def scan(part):
        cols = pl.ds(part * half * chunk, half * chunk)

        def state_copy(slot, source, k):
            return pltpu.make_async_remote_copy(
                src_ref=sent.at[source, :, cols],
                dst_ref=got.at[slot, :, cols],
                send_sem=st_send.at[part, slot],
                recv_sem=st_recv.at[part, slot],
                device_id={"context": lax.rem(here + k, n_ctx)},
                device_id_type=MESH,
            )

        rates = rate[:, cols]
        sent[0, :, cols] = end[:, cols].astype(BF16)
        copies = [state_copy(0, 0, 1), state_copy(1, 0, 2)]
        for copy in copies:
            copy.start()
        yield
        for copy in copies:
            copy.wait_recv()
        now = got[0, :, cols].astype(F32) * present(1)
        now = now + jnp.exp(-rates * rows) * (got[1, :, cols].astype(F32) * present(2))
        for i, span in enumerate(spans):
            state[:, cols] = now
            sent[i + 1, :, cols] = now.astype(BF16)
            copy = state_copy(i + 2, i + 1, span)
            copy.start()
            copies.append(copy)
            yield
            copy.wait_recv()
            now = state[:, cols] + jnp.exp(-rates * (rows * span)) * (got[i + 2, :, cols].astype(F32) * present(span))
        state[:, cols] = now * amp[:, cols] * jnp.exp(-rates)
        for copy in copies:
            copy.wait_send()

    def run(body, first_chunk, last_chunk):
        if first_chunk < last_chunk:
            pl.loop(first_chunk, last_chunk)(body)

    def filter_and_next(c):
        short(c)
        spectra(c + 1)
        ends(c)

    spectra(0)
    for load in loads[7:12]:
        load.wait()
    run(filter_and_next, 0, half)
    early, late = scan(0), scan(1)
    next(early, None)
    run(filter_and_next, half, chunks - 1)
    next(early, None)
    short(chunks - 1)
    ends(chunks - 1)
    next(late, None)
    for load in loads[12:]:
        load.wait()
    run(local_long, 0, half)
    next(early, None)
    next(late, None)
    run(local_long, half, chunks)
    for _ in early:
        pass
    next(late, None)
    power[...] = jnp.zeros_like(power)
    run(carry, 0, half)
    for _ in late:
        pass
    run(carry, half, chunks)

    pow_row[...] = lax.dot_general(
        jnp.ones((SUB, LANES), F32),
        power[...],
        (((1,), (1,)), ((), ())),
        precision=lax.Precision.HIGHEST,
        preferred_element_type=F32,
    )
    shares = [
        pltpu.make_async_remote_copy(
            src_ref=pow_row,
            dst_ref=pow_got.at[k - 1],
            send_sem=pow_send.at[k - 1],
            recv_sem=pow_recv.at[k - 1],
            device_id={"channel": lax.rem(lane_group + k, n_chan)},
            device_id_type=MESH,
        )
        for k in range(1, n_chan)
    ]
    for copy in shares:
        copy.start()

    @pl.loop(0, chunks)
    def _(c):
        halo_copy(c).wait_send()

    for copy in shares:
        copy.wait()
    whole = pow_row[...]
    for k in range(n_chan - 1):
        whole = whole + pow_got[k]
    power_out[...] = whole


def on_device(channels, first_stream, value_stream, short_gate, out_gate, mr_filter, li_residue, li_rate, li_skip, norm_gain):
    rows, width = first_stream.shape
    taps, poles = mr_filter.shape[0], li_residue.shape[0]
    chunk = min(512, width // 2)
    chunks = width // chunk
    short_n, long_n = rows + taps, 2 * rows
    fs, fsh, gs = transforms(short_n, taps, rows, taps)
    fl, flh, gl = transforms(long_n, 0, rows, rows)
    fl = np.concatenate([fl[:, :rows], fl[:, long_n : long_n + rows]], 1)
    n_ctx, n_chan = lax.axis_size("context"), lax.axis_size("channel")
    rounds = 1
    while 1 << rounds < n_ctx:
        rounds += 1
    operands = (first_stream, value_stream, short_gate, out_gate, mr_filter, li_residue, li_rate, li_skip[None, :], fs, gs, fsh, flh, fl, gl)
    vmem, dma = pltpu.VMEM, pltpu.SemaphoreType.DMA
    shape = jax.ShapeDtypeStruct
    long_out, power = pl.pallas_call(
        functools.partial(fused_kernel, n_ctx, n_chan, chunk),
        in_specs=[pl.BlockSpec(memory_space=pltpu.HBM)] * len(operands),
        out_specs=[pl.BlockSpec(memory_space=pltpu.VMEM)] * 2,
        out_shape=[shape((rows, width), BF16), shape((SUB, rows), F32)],
        scratch_shapes=[vmem(a.shape, a.dtype) for a in operands]
        + [
            vmem((short_n, width), BF16),
            vmem((short_n, width), F32),
            vmem((long_n, width), F32),
            vmem((rows, chunk), F32),
            vmem((rows, width), BF16),
            vmem((rows, width), F32),
            vmem((rows, LANES), F32),
            vmem((poles, width), F32),
            vmem((rounds, poles, width), BF16),
            vmem((rounds + 1, poles, width), BF16),
            vmem((poles, width), F32),
            vmem((rows, LANES), F32),
            vmem((SUB, rows), F32),
            vmem((n_chan - 1, SUB, rows), F32),
            vmem((poles, width), F32),
            vmem((poles, width), F32),
            vmem((poles, SUB, width), F32),
            dma((len(operands) + 2,)),
            dma((chunks,)),
            dma((chunks,)),
            dma((2, rounds + 1)),
            dma((2, rounds + 1)),
            dma((n_chan - 1,)),
            dma((n_chan - 1,)),
        ],
        compiler_params=pltpu.CompilerParams(
            collective_id=0, has_side_effects=True, vmem_limit_bytes=56 * 1024 * 1024
        ),
        cost_estimate=pl.CostEstimate(flops=int(8e9), bytes_accessed=int(8e6), transcendentals=0),
        name="filters",
    )(*operands)
    scale = lax.rsqrt(power[0] / channels + 1e-06)
    gated = out_gate.astype(F32) * long_out.astype(F32)
    return (gated * scale[:, None] * norm_gain[None, :]).astype(BF16)


def solution(mesh):
    both, columns, channel = P("context", "channel"), P(None, "channel"), P("channel")

    def whole_arrays(*args):
        body = functools.partial(on_device, args[0].shape[1])
        return jax.shard_map(
            body,
            mesh=mesh,
            in_specs=(both,) * 4 + (columns,) * 3 + (channel,) * 2,
            out_specs=both,
            check_vma=False,
        )(*args)

    return whole_arrays
```

profile of v0, /device:TPU:0, one launch (start us, length us, event | category | flops | bytes accessed | tf_op | source)
XLA Modules:
  0.0 41.9 jit_solution(11225539238172656671)
XLA Ops:
  0.0 0.0 copy-start
  0.0 0.0 copy-start.1
  0.0 38.6 %filters.1 = (bf16[256,2048]{1,0:T(8,128)(2,1)}, f32[8,256]{1,0:T(8,128)}) custom-call(bf16[256,2048]{1,0:T(8,128)(2,1)} %refs_0_.1, bf16[256,2048]{1,0:T(8,128)(2,1)} %refs_1_.1, bf16[256,2048]{1,0:T(8,128)(2,1)} %refs_2_.1, bf16[256,2048]{1,0:T(8,128)(2,1)} %refs_3_.1, f32[128,2048]{1,0:T(8,128)} %refs_4_.1, f32[16,2048]{1,0:T(8,128)} %refs_5_.1, ...), custom_call_target="tpu_custom_call" | custom-call | flops 8000000000 | bytes 8000000 | tf_op jit(solution)/shard_map/filters/pallas_call | solution.py:340
  38.6 0.7 %add_rsqrt_fusion = f32[1,256]{1,0:T(1,128)S(1)} fusion(f32[8,256]{1,0:T(8,128)} %get-tuple-element.8), kind=kLoop, calls=%fused_computation.1 | loop fusion | flops 512 | bytes 2048 | tf_op jit(solution)/shard_map/rsqrt | solution.py:378
  39.3 0.0 copy-done
  39.3 0.0 copy-done.1
  39.3 2.6 %multiply_convert_fusion = bf16[256,2048]{1,0:T(8,128)(2,1)} fusion(bf16[256,2048]{1,0:T(8,128)(2,1)} %get-tuple-element.7, bf16[256,2048]{1,0:T(8,128)(2,1)S(1)} %copy-done, f32[2048]{0:T(1024)S(1)} %copy-done.1, f32[256]{0:T(256)S(1)} %bitcast.2), kind=kLoop, calls=%fused_computation | loop fusion | flops 3145728 | bytes 3154944 | tf_op jit(solution)/shard_map/convert_element_type | solution.py:380
Async XLA Ops:
  0.0 39.3 %copy-start = (bf16[256,2048]{1,0:T(8,128)(2,1)S(1)}, bf16[256,2048]{1,0:T(8,128)(2,1)}, u32[]{:S(2)}) copy-start(bf16[256,2048]{1,0:T(8,128)(2,1)} %refs_3_.1) | copy-start | bytes 3145732
  0.0 39.3 %copy-start.1 = (f32[2048]{0:T(1024)S(1)}, f32[2048]{0:T(1024)}, u32[]{:S(2)}) copy-start(f32[2048]{0:T(1024)} %param.23) | copy-start | bytes 24580
where the time goes:
time: 42.1 us; the launch traced here: 41.9 us
  Pallas kernels  38.6 us (92%)
  other arithmetic  3.29 us (8%)
    pallas_call x1, Pallas kernels, on_device(): pl.pallas_call(functools.partial(fused_kernel, n_ctx, n_chan, chunk), in_...  38.6 us
    convert_element_type x1, other arithmetic, on_device(): return (gated * scale[:, None] * norm_gain[None, :]).astype(BF16)  2.58 us

commit v1 on v0

--- a/solution.py
+++ b/solution.py
@@ -20,16 +20,26 @@
     return hi, lo
 
 
-def transforms(points, out_first, out_count, taps):
-    freq = 2.0 * np.pi * (np.arange(points // 2) + 0.5) / points
-    phase = freq[:, None] * np.arange(points)[None, :]
+def transforms(block):
+    points = 2 * block
+    order = np.concatenate([np.arange(0, block, 2), np.arange(1, block, 2)])
+    phase = 2.0 * np.pi / points * (order + 0.5)[:, None] * np.arange(points)[None, :]
     full = np.concatenate([np.cos(phase), np.sin(phase)], 0)
-    hi, lo = split_const(full[:, :taps])
-    taps_m = np.concatenate([hi, hi, lo], 1)
-    hi, lo = split_const(full)
-    both = np.concatenate([hi, lo], 1)
-    back = full[:, out_first : out_first + out_count].T * (2.0 / points)
-    return both, taps_m, back.astype(BF16)
+    hi, lo = split_const(full[:, :block])
+    back = (full.T * (2.0 / points)).astype(BF16)
+    return np.concatenate([hi, lo, hi], 1), back[:block], back[block:]
+
+
+def plus_later(x, later):
+    q = x.shape[0] // 4
+    a, b, c, d = (x[i * q : (i + 1) * q] for i in range(4))
+    e, f, g, h = (later[i * q : (i + 1) * q] for i in range(4))
+    return jnp.concatenate([a - g, b + h, c + e, d - f], 0)
+
+
+def twice(v):
+    v = v.astype(BF16)
+    return jnp.concatenate([v, v], 0)
 
 
 def dot(a, b):
@@ -39,7 +49,7 @@
 def three(v):
     hi = v.astype(BF16)
     lo = (v - hi.astype(F32)).astype(BF16)
-    return jnp.concatenate([hi, lo, hi], 0)
+    return jnp.concatenate([hi, hi, lo], 0)
 
 
 def times_spectrum(x, h):
@@ -70,10 +80,10 @@
 
 
 def fused_kernel(n_ctx, n_chan, chunk, *refs):
-    n_in = 14
-    (first_h, value_h, gate_h, og_h, filt_h, res_h, rate_h, skip_h, fs_h, gs_h, fsh_h, flh_h, fl_h, gl_h) = refs[:n_in]
+    n_in = 11
+    (first_h, value_h, gate_h, og_h, filt_h, res_h, rate_h, skip_h, fwd_h, back0_h, back1_h) = refs[:n_in]
     long_out, power_out = refs[n_in : n_in + 2]
-    (first, value, gate, og, filt, res, rate, skip, fs, gs, fsh, flh, fl, gl) = refs[n_in + 2 : 2 * n_in + 2]
+    (first, value, gate, og, filt, res, rate, skip, fwd, back0, back1) = refs[n_in + 2 : 2 * n_in + 2]
     (x, hs, hl, impulse, mixed, base, total, end, sent, got, state, power, pow_row, pow_got, amp, step8, fade) = refs[
         2 * n_in + 2 : 2 * n_in + 19
     ]
@@ -88,19 +98,16 @@
     pairs = [
         (first_h.at[tail], first.at[tail]),
         (value_h.at[tail], value.at[tail]),
-        (filt_h, filt),
-        (fsh_h, fsh),
         (res_h, res),
         (rate_h, rate),
-        (flh_h, flh),
+        (filt_h, filt),
+        (fwd_h, fwd),
         (first_h.at[head], first.at[head]),
         (value_h.at[head], value.at[head]),
-        (fs_h, fs),
-        (gs_h, gs),
+        (back1_h, back1),
         (gate_h, gate),
         (skip_h, skip),
-        (fl_h, fl),
-        (gl_h, gl),
+        (back0_h, back0),
         (og_h, og),
     ]
     loads = [pltpu.make_async_copy(a, b, in_sem.at[i]) for i, (a, b) in enumerate(pairs)]
@@ -143,7 +150,7 @@
         x[pl.ds(rows, taps), cols] = product(tail, cols)
         halo_copy(c).start()
 
-    for load in loads[2:7]:
+    for load in loads[2:6]:
         load.wait()
     amp[...] = res[...] * jnp.sqrt(2.0 * rate[...])
     step8[...] = jnp.exp(-SUB * rate[...])
@@ -174,17 +181,23 @@
                 impulse[a * SUB : (a + 1) * SUB, t * LANES : (t + 1) * LANES] = v
 
             mode_sums(start, steps(lanes), rows // SUB, put)
-        hs[:, cols] = dot(fsh[...], three(filt[:, cols]))
-        hl[:, cols] = dot(flh[...], three(impulse[...]))
+        hs[:, cols] = dot(fwd[...], three(filt[:, cols]))
+        early_h = dot(fwd[:, : 2 * taps], twice(impulse[:taps]))
+        hl[: 2 * taps, cols] = early_h
+        hl[2 * taps :, cols] = plus_later(early_h, dot(fwd[:, : 2 * taps], twice(impulse[taps:])))
 
     def short(c):
         cols = at_chunk(c)
         halo_copy(c).wait_recv()
         before = (x[pl.ds(0, taps), cols].astype(F32) * present(1)).astype(BF16)
-        window = jnp.concatenate([before, product(head, cols), x[pl.ds(rows, taps), cols]], 0)
-        y = times_spectrum(dot(fs[...], jnp.concatenate([window, window], 0)), hs[:, cols])
-        out = dot(gs[...], y.astype(BF16))
-        mixed[:, cols] = (gate[:, cols].astype(F32) * out).astype(BF16)
+        parts = [before, product(head, cols), x[pl.ds(rows, taps), cols]]
+        parts = [dot(fwd[:, : 2 * taps], twice(p)) for p in parts]
+        h = hs[:, cols]
+        for i in range(2):
+            y = times_spectrum(plus_later(parts[i], parts[i + 1]), h)
+            out = dot(back1[...], y.astype(BF16))
+            span = pl.ds(i * taps, taps)
+            mixed[span, cols] = (gate[span, cols].astype(F32) * out).astype(BF16)
 
     def ends(c):
         for lanes in lane_tiles(c):
@@ -200,9 +213,13 @@
 
     def local_long(c):
         cols = at_chunk(c)
-        here_x = mixed[:, cols]
-        y = times_spectrum(dot(fl[...], jnp.concatenate([here_x, here_x], 0)), hl[:, cols])
-        base[:, cols] = dot(gl[...], y.astype(BF16)) + skip[:, cols] * here_x.astype(F32)
+        x0, x1 = mixed[:taps, cols], mixed[taps:, cols]
+        y0, y1 = dot(fwd[:, : 2 * taps], twice(x0)), dot(fwd[:, : 2 * taps], twice(x1))
+        h0, h1 = hl[: 2 * taps, cols], hl[2 * taps :, cols]
+        later = times_spectrum(y0, h1) + times_spectrum(plus_later(jnp.zeros_like(y1), y1), h0)
+        gain = skip[:, cols]
+        base[:taps, cols] = dot(back0[...], times_spectrum(y0, h0).astype(BF16)) + gain * x0.astype(F32)
+        base[taps:, cols] = dot(back1[...], later.astype(BF16)) + gain * x1.astype(F32)
 
     def carry(c):
         for lanes in lane_tiles(c):
@@ -263,7 +280,7 @@
         ends(c)
 
     spectra(0)
-    for load in loads[7:12]:
+    for load in loads[6:10]:
         load.wait()
     run(filter_and_next, 0, half)
     early, late = scan(0), scan(1)
@@ -273,7 +290,7 @@
     short(chunks - 1)
     ends(chunks - 1)
     next(late, None)
-    for load in loads[12:]:
+    for load in loads[10:]:
         load.wait()
     run(local_long, 0, half)
     next(early, None)
@@ -327,14 +344,13 @@
     chunk = min(512, width // 2)
     chunks = width // chunk
     short_n, long_n = rows + taps, 2 * rows
-    fs, fsh, gs = transforms(short_n, taps, rows, taps)
-    fl, flh, gl = transforms(long_n, 0, rows, rows)
-    fl = np.concatenate([fl[:, :rows], fl[:, long_n : long_n + rows]], 1)
+    assert rows == 2 * taps
+    fwd, back0, back1 = transforms(taps)
     n_ctx, n_chan = lax.axis_size("context"), lax.axis_size("channel")
     rounds = 1
     while 1 << rounds < n_ctx:
         rounds += 1
-    operands = (first_stream, value_stream, short_gate, out_gate, mr_filter, li_residue, li_rate, li_skip[None, :], fs, gs, fsh, flh, fl, gl)
+    operands = (first_stream, value_stream, short_gate, out_gate, mr_filter, li_residue, li_rate, li_skip[None, :], fwd, back0, back1)
     vmem, dma = pltpu.VMEM, pltpu.SemaphoreType.DMA
     shape = jax.ShapeDtypeStruct
     long_out, power = pl.pallas_call(
@@ -345,7 +361,7 @@
         scratch_shapes=[vmem(a.shape, a.dtype) for a in operands]
         + [
             vmem((short_n, width), BF16),
-            vmem((short_n, width), F32),
+            vmem((rows, width), F32),
             vmem((long_n, width), F32),
             vmem((rows, chunk), F32),
             vmem((rows, width), BF16),
@@ -370,7 +386,7 @@
             dma((n_chan - 1,)),
         ],
         compiler_params=pltpu.CompilerParams(
-            collective_id=0, has_side_effects=True, vmem_limit_bytes=56 * 1024 * 1024
+            collective_id=0, has_side_effects=True, vmem_limit_bytes=40 * 1024 * 1024
         ),
         cost_estimate=pl.CostEstimate(flops=int(8e9), bytes_accessed=int(8e6), transcendentals=0),
         name="filters",

time: 42.1 us -> 51 us (1.21)
  local copies, waits for them, and re-layouts: 0.01 us -> 11.2 us
  other arithmetic: 3.29 us -> 1.48 us
  Pallas kernels: 38.6 us -> 37.7 us
    unnamed x4 -> x24, local copies, waits for them, and re-layouts: 0.01 us -> 11.2 us
    convert_element_type x1, other arithmetic: 2.58 us -> 1.47 us  [on_device(): return (gated * scale[:, None] * norm_gain[None, :]).astype(BF16)]
    pallas_call x1, Pallas kernels: 38.6 us -> 37.7 us  [on_device(): pl.pallas_call(functools.partial(fused_kernel, n_ctx, n_chan, chunk), in_...]
    rsqrt x1, other arithmetic: 0.7 us -> 0.01 us  [on_device(): scale = lax.rsqrt(power[0] / channels + 1e-06)]
where the time goes in v1:
time: 51 us; the launch traced here: 50.5 us
  Pallas kernels  37.7 us (74%)
  local copies, waits for them, and re-layouts  11.2 us (22%)
  other arithmetic  1.48 us (3%)
    pallas_call x1, Pallas kernels, on_device(): pl.pallas_call(functools.partial(fused_kernel, n_ctx, n_chan, chunk), in_...  37.7 us
    unnamed x24, local copies, waits for them, and re-layouts  11.2 us
    convert_element_type x1, other arithmetic, on_device(): return (gated * scale[:, None] * norm_gain[None, :]).astype(BF16)  1.47 us

profile of v1, /device:TPU:0, one launch (start us, length us, event | category | flops | bytes accessed | tf_op | source)
XLA Modules:
  0.0 50.5 jit_solution(3605951438888828116)
XLA Ops:
  0.0 0.0 copy-start
  0.0 1.2 %copy-done = bf16[256,2048]{1,0:T(8,128)(2,1)S(1)} copy-done((bf16[256,2048]{1,0:T(8,128)(2,1)S(1)}, bf16[256,2048]{1,0:T(8,128)(2,1)}, u32[]{:S(2)}) %copy-start) | copy-done | bytes 1048600
  1.2 0.0 copy-start.1
  1.2 1.2 %copy-done.1 = bf16[256,2048]{1,0:T(8,128)(2,1)S(1)} copy-done((bf16[256,2048]{1,0:T(8,128)(2,1)S(1)}, bf16[256,2048]{1,0:T(8,128)(2,1)}, u32[]{:S(2)}) %copy-start.1) | copy-done | bytes 1048600
  2.5 0.0 copy-start.2
  2.5 1.2 %copy-done.2 = bf16[256,2048]{1,0:T(8,128)(2,1)S(1)} copy-done((bf16[256,2048]{1,0:T(8,128)(2,1)S(1)}, bf16[256,2048]{1,0:T(8,128)(2,1)}, u32[]{:S(2)}) %copy-start.2) | copy-done | bytes 1048600
  3.7 0.0 copy-start.3
  3.7 1.2 %copy-done.3 = bf16[256,2048]{1,0:T(8,128)(2,1)S(1)} copy-done((bf16[256,2048]{1,0:T(8,128)(2,1)S(1)}, bf16[256,2048]{1,0:T(8,128)(2,1)}, u32[]{:S(2)}) %copy-start.3) | copy-done | bytes 1048600
  4.9 0.0 copy-start.4
  4.9 1.2 %copy-done.4 = f32[128,2048]{1,0:T(8,128)S(1)} copy-done((f32[128,2048]{1,0:T(8,128)S(1)}, f32[128,2048]{1,0:T(8,128)}, u32[]{:S(2)}) %copy-start.4) | copy-done | bytes 1048600
  6.1 0.0 copy-start.5
  6.1 0.9 %copy-done.5 = f32[16,2048]{1,0:T(8,128)S(1)} copy-done((f32[16,2048]{1,0:T(8,128)S(1)}, f32[16,2048]{1,0:T(8,128)}, u32[]{:S(2)}) %copy-start.5) | copy-done | bytes 131096
  7.0 0.0 copy-start.6
  7.0 0.9 %copy-done.6 = f32[16,2048]{1,0:T(8,128)S(1)} copy-done((f32[16,2048]{1,0:T(8,128)S(1)}, f32[16,2048]{1,0:T(8,128)}, u32[]{:S(2)}) %copy-start.6) | copy-done | bytes 131096
  7.9 0.0 copy-start.7
  7.9 0.7 %copy-done.7 = f32[2048]{0:T(1024)S(1)} copy-done((f32[2048]{0:T(1024)S(1)}, f32[2048]{0:T(1024)}, u32[]{:S(2)}) %copy-start.7) | copy-done | bytes 8216
  8.6 0.0 copy-start.8
  8.6 0.9 %copy-done.8 = bf16[256,384]{1,0:T(8,128)(2,1)S(1)} copy-done((bf16[256,384]{1,0:T(8,128)(2,1)S(1)}, bf16[256,384]{1,0:T(8,128)(2,1)}, u32[]{:S(2)}) %copy-start.8) | copy-done | bytes 196632
  9.6 0.0 copy-start.9
  9.6 0.8 %copy-done.9 = bf16[128,256]{1,0:T(8,128)(2,1)S(1)} copy-done((bf16[128,256]{1,0:T(8,128)(2,1)S(1)}, bf16[128,256]{1,0:T(8,128)(2,1)}, u32[]{:S(2)}) %copy-start.9) | copy-done | bytes 65560
  10.4 0.8 %copy-done.10 = bf16[128,256]{1,0:T(8,128)(2,1)S(1)} copy-done((bf16[128,256]{1,0:T(8,128)(2,1)S(1)}, bf16[128,256]{1,0:T(8,128)(2,1)}, u32[]{:S(2)}) %copy-start.10) | copy-done | bytes 65560
  11.2 37.7 %filters.1 = (bf16[256,2048]{1,0:T(8,128)(2,1)S(1)}, f32[8,256]{1,0:T(8,128)S(1)}) custom-call(bf16[256,2048]{1,0:T(8,128)(2,1)S(1)} %copy-done.1, bf16[256,2048]{1,0:T(8,128)(2,1)S(1)} %copy-done.2, bf16[256,2048]{1,0:T(8,128)(2,1)S(1)} %copy-done.3, bf16[256,2048]{1,0:T(8,128)(2,1)S(1)} %copy-done, f32[128,2048]{1,0:T(8,128)S(1)} %copy-done.4, ...), custom_call_target="tpu_custom_call" | custom-call | flops 8000000000 | bytes 8000000 | tf_op jit(solution)/shard_map/filters/pallas_call | solution.py:356
  49.0 0.0 copy-done.11
  49.0 1.5 %multiply_convert_fusion = bf16[256,2048]{1,0:T(8,128)(2,1)} fusion(bf16[256,2048]{1,0:T(8,128)(2,1)S(1)} %get-tuple-element.7, bf16[256,2048]{1,0:T(8,128)(2,1)S(1)} %copy-done, f32[2048]{0:T(1024)S(1)} %copy-done.11, f32[256]{0:T(256)S(1)} %bitcast.3), kind=kLoop, calls=%fused_computation | loop fusion | flops 3145728 | bytes 3154944 | tf_op jit(solution)/shard_map/convert_element_type | solution.py:396
  (3 shorter events, 0.0 us)
Async XLA Ops:
  0.0 1.2 %copy-start = (bf16[256,2048]{1,0:T(8,128)(2,1)S(1)}, bf16[256,2048]{1,0:T(8,128)(2,1)}, u32[]{:S(2)}) copy-start(bf16[256,2048]{1,0:T(8,128)(2,1)} %refs_3_.1) | copy-start | bytes 3145732
  1.2 1.2 %copy-start.1 = (bf16[256,2048]{1,0:T(8,128)(2,1)S(1)}, bf16[256,2048]{1,0:T(8,128)(2,1)}, u32[]{:S(2)}) copy-start(bf16[256,2048]{1,0:T(8,128)(2,1)} %refs_0_.1) | copy-start | bytes 3145732
  2.5 1.2 %copy-start.2 = (bf16[256,2048]{1,0:T(8,128)(2,1)S(1)}, bf16[256,2048]{1,0:T(8,128)(2,1)}, u32[]{:S(2)}) copy-start(bf16[256,2048]{1,0:T(8,128)(2,1)} %refs_1_.1) | copy-start | bytes 3145732
  3.7 1.2 %copy-start.3 = (bf16[256,2048]{1,0:T(8,128)(2,1)S(1)}, bf16[256,2048]{1,0:T(8,128)(2,1)}, u32[]{:S(2)}) copy-start(bf16[256,2048]{1,0:T(8,128)(2,1)} %refs_2_.1) | copy-start | bytes 3145732
  4.9 1.2 %copy-start.4 = (f32[128,2048]{1,0:T(8,128)S(1)}, f32[128,2048]{1,0:T(8,128)}, u32[]{:S(2)}) copy-start(f32[128,2048]{1,0:T(8,128)} %refs_4_.1) | copy-start | bytes 3145732
  6.1 0.9 %copy-start.5 = (f32[16,2048]{1,0:T(8,128)S(1)}, f32[16,2048]{1,0:T(8,128)}, u32[]{:S(2)}) copy-start(f32[16,2048]{1,0:T(8,128)} %refs_5_.1) | copy-start | bytes 393220
  7.0 0.9 %copy-start.6 = (f32[16,2048]{1,0:T(8,128)S(1)}, f32[16,2048]{1,0:T(8,128)}, u32[]{:S(2)}) copy-start(f32[16,2048]{1,0:T(8,128)} %refs_6_.1) | copy-start | bytes 393220
  7.9 0.7 %copy-start.7 = (f32[2048]{0:T(1024)S(1)}, f32[2048]{0:T(1024)}, u32[]{:S(2)}) copy-start(f32[2048]{0:T(1024)} %param.19) | copy-start | bytes 24580
  8.6 0.9 %copy-start.8 = (bf16[256,384]{1,0:T(8,128)(2,1)S(1)}, bf16[256,384]{1,0:T(8,128)(2,1)}, u32[]{:S(2)}) copy-start(bf16[256,384]{1,0:T(8,128)(2,1)} %constant.11.clone.refs_8_) | copy-start | bytes 589828
  9.6 0.8 %copy-start.9 = (bf16[128,256]{1,0:T(8,128)(2,1)S(1)}, bf16[128,256]{1,0:T(8,128)(2,1)}, u32[]{:S(2)}) copy-start(bf16[128,256]{1,0:T(8,128)(2,1)} %constant.13.clone.refs_10_) | copy-start | bytes 196612
  10.4 0.8 %copy-start.10 = (bf16[128,256]{1,0:T(8,128)(2,1)S(1)}, bf16[128,256]{1,0:T(8,128)(2,1)}, u32[]{:S(2)}) copy-start(bf16[128,256]{1,0:T(8,128)(2,1)} %constant.12.clone.refs_9_) | copy-start | bytes 196612
  11.2 37.8 %copy-start.11 = (f32[2048]{0:T(1024)S(1)}, f32[2048]{0:T(1024)}, u32[]{:S(2)}) copy-start(f32[2048]{0:T(1024)} %param.20) | copy-start | bytes 24580

commit v2 on v1

--- a/solution.py
+++ b/solution.py
@@ -79,15 +79,23 @@
 MESH = pl.DeviceIdType.MESH
 
 
+def scan_plan(count):
+    plan, window = [[1, 2]], 2
+    while window < count:
+        plan.append([k * window for k in (1, 2, 3) if k * window < count])
+        window *= 4
+    return plan
+
+
 def fused_kernel(n_ctx, n_chan, chunk, *refs):
     n_in = 11
     (first_h, value_h, gate_h, og_h, filt_h, res_h, rate_h, skip_h, fwd_h, back0_h, back1_h) = refs[:n_in]
     long_out, power_out = refs[n_in : n_in + 2]
     (first, value, gate, og, filt, res, rate, skip, fwd, back0, back1) = refs[n_in + 2 : 2 * n_in + 2]
-    (x, hs, hl, impulse, mixed, base, total, end, sent, got, state, power, pow_row, pow_got, amp, step8, fade) = refs[
-        2 * n_in + 2 : 2 * n_in + 19
+    (x, hs, hl, impulse, mixed, base, total, end, sent, got, state, power, pow_row, pow_got, amp, step8, fade, out_buf) = refs[
+        2 * n_in + 2 : 2 * n_in + 20
     ]
-    in_sem, halo_send, halo_recv, st_send, st_recv, pow_send, pow_recv = refs[2 * n_in + 19 :]
+    in_sem, halo_send, halo_recv, st_send, st_recv, pow_send, pow_recv, out_sem = refs[2 * n_in + 20 :]
 
     rows, width = first.shape
     taps = filt.shape[0]
@@ -111,13 +119,11 @@
         (og_h, og),
     ]
     loads = [pltpu.make_async_copy(a, b, in_sem.at[i]) for i, (a, b) in enumerate(pairs)]
-    for load in loads:
+    for load in loads[:2]:
         load.start()
 
-    spans = []
-    while 2 << len(spans) < n_ctx:
-        spans.append(2 << len(spans))
-    offsets = sorted({k % n_ctx for s in [1, 2] + spans for k in (s, -s)} - {0})
+    plan = scan_plan(n_ctx)
+    offsets = sorted({k % n_ctx for shifts in plan for s in shifts for k in (s, -s)} - {0})
     barrier = pltpu.get_barrier_semaphore()
     for k in offsets:
         pl.semaphore_signal(barrier, inc=1, device_id={"context": lax.rem(here + k, n_ctx)}, device_id_type=MESH)
@@ -125,6 +131,8 @@
         pl.semaphore_signal(barrier, inc=1, device_id={"channel": lax.rem(lane_group + k, n_chan)}, device_id_type=MESH)
     loads[0].wait()
     loads[1].wait()
+    for load in loads[2:]:
+        load.start()
     pl.semaphore_wait(barrier, len(offsets) + n_chan - 1)
 
     def at_chunk(c):
@@ -157,7 +165,7 @@
 
     sub = sublane_index()
     poles = rate.shape[0]
-    half = chunks // 2
+    half = chunks - 1
 
     def lane_tiles(c):
         return [pl.ds(pl.multiple_of(c * chunk + t, LANES), LANES) for t in range(0, chunk, LANES)]
@@ -230,45 +238,42 @@
 
             mode_sums(start, steps(lanes), rows // SUB, put)
             out = (base[:, lanes] + total[...]).astype(BF16)
-            long_out[:, lanes] = out
+            out_buf[:, lanes] = out
             gated = og[:, lanes].astype(F32) * out.astype(F32)
             power[...] += gated * gated
 
     def scan(part):
-        cols = pl.ds(part * half * chunk, half * chunk)
-
-        def state_copy(slot, source, k):
-            return pltpu.make_async_remote_copy(
-                src_ref=sent.at[source, :, cols],
-                dst_ref=got.at[slot, :, cols],
-                send_sem=st_send.at[part, slot],
-                recv_sem=st_recv.at[part, slot],
-                device_id={"context": lax.rem(here + k, n_ctx)},
-                device_id_type=MESH,
-            )
-
+        cols = pl.ds(part * half * chunk, (chunks - half if part else half) * chunk)
         rates = rate[:, cols]
-        sent[0, :, cols] = end[:, cols].astype(BF16)
-        copies = [state_copy(0, 0, 1), state_copy(1, 0, 2)]
-        for copy in copies:
-            copy.start()
-        yield
-        for copy in copies:
-            copy.wait_recv()
-        now = got[0, :, cols].astype(F32) * present(1)
-        now = now + jnp.exp(-rates * rows) * (got[1, :, cols].astype(F32) * present(2))
-        for i, span in enumerate(spans):
+        now, copies, slot = end[:, cols], [], 0
+        for i, shifts in enumerate(plan):
+            sent[i, :, cols] = now.astype(BF16)
             state[:, cols] = now
-            sent[i + 1, :, cols] = now.astype(BF16)
-            copy = state_copy(i + 2, i + 1, span)
-            copy.start()
-            copies.append(copy)
+            for j, k in enumerate(shifts):
+                copy = pltpu.make_async_remote_copy(
+                    src_ref=sent.at[i, :, cols],
+                    dst_ref=got.at[slot + j, :, cols],
+                    send_sem=st_send.at[part, slot + j],
+                    recv_sem=st_recv.at[part, slot + j],
+                    device_id={"context": lax.rem(here + k, n_ctx)},
+                    device_id_type=MESH,
+                )
+                copy.start()
+                copies.append(copy)
             yield
-            copy.wait_recv()
-            now = state[:, cols] + jnp.exp(-rates * (rows * span)) * (got[i + 2, :, cols].astype(F32) * present(span))
+            now = state[:, cols] if i else jnp.zeros_like(rates)
+            for j, k in enumerate(shifts):
+                copies[slot + j].wait_recv()
+                faded = jnp.exp(-rates * (rows * (k if i else k - 1)))
+                now = now + faded * (got[slot + j, :, cols].astype(F32) * present(k))
+            slot += len(shifts)
         state[:, cols] = now * amp[:, cols] * jnp.exp(-rates)
         for copy in copies:
             copy.wait_send()
+
+    def write_back(part):
+        cols = pl.ds(part * half * chunk, (chunks - half if part else half) * chunk)
+        return pltpu.make_async_copy(out_buf.at[:, cols], long_out.at[:, cols], out_sem.at[part])
 
     def run(body, first_chunk, last_chunk):
         if first_chunk < last_chunk:
@@ -285,25 +290,24 @@
     run(filter_and_next, 0, half)
     early, late = scan(0), scan(1)
     next(early, None)
-    run(filter_and_next, half, chunks - 1)
-    next(early, None)
     short(chunks - 1)
     ends(chunks - 1)
     next(late, None)
+    next(early, None)
     for load in loads[10:]:
         load.wait()
     run(local_long, 0, half)
-    next(early, None)
     next(late, None)
     run(local_long, half, chunks)
     for _ in early:
         pass
-    next(late, None)
     power[...] = jnp.zeros_like(power)
     run(carry, 0, half)
+    write_back(0).start()
     for _ in late:
         pass
     run(carry, half, chunks)
+    write_back(1).start()
 
     pow_row[...] = lax.dot_general(
         jnp.ones((SUB, LANES), F32),
@@ -336,6 +340,8 @@
     for k in range(n_chan - 1):
         whole = whole + pow_got[k]
     power_out[...] = whole
+    write_back(0).wait()
+    write_back(1).wait()
 
 
 def on_device(channels, first_stream, value_stream, short_gate, out_gate, mr_filter, li_residue, li_rate, li_skip, norm_gain):
@@ -347,16 +353,15 @@
     assert rows == 2 * taps
     fwd, back0, back1 = transforms(taps)
     n_ctx, n_chan = lax.axis_size("context"), lax.axis_size("channel")
-    rounds = 1
-    while 1 << rounds < n_ctx:
-        rounds += 1
+    plan = scan_plan(n_ctx)
+    rounds, slots = len(plan), sum(len(shifts) for shifts in plan)
     operands = (first_stream, value_stream, short_gate, out_gate, mr_filter, li_residue, li_rate, li_skip[None, :], fwd, back0, back1)
     vmem, dma = pltpu.VMEM, pltpu.SemaphoreType.DMA
     shape = jax.ShapeDtypeStruct
     long_out, power = pl.pallas_call(
         functools.partial(fused_kernel, n_ctx, n_chan, chunk),
         in_specs=[pl.BlockSpec(memory_space=pltpu.HBM)] * len(operands),
-        out_specs=[pl.BlockSpec(memory_space=pltpu.VMEM)] * 2,
+        out_specs=[pl.BlockSpec(memory_space=pltpu.HBM), pl.BlockSpec(memory_space=pltpu.VMEM)],
         out_shape=[shape((rows, width), BF16), shape((SUB, rows), F32)],
         scratch_shapes=[vmem(a.shape, a.dtype) for a in operands]
         + [
@@ -369,7 +374,7 @@
             vmem((rows, LANES), F32),
             vmem((poles, width), F32),
             vmem((rounds, poles, width), BF16),
-            vmem((rounds + 1, poles, width), BF16),
+            vmem((slots, poles, width), BF16),
             vmem((poles, width), F32),
             vmem((rows, LANES), F32),
             vmem((SUB, rows), F32),
@@ -377,16 +382,18 @@
             vmem((poles, width), F32),
             vmem((poles, width), F32),
             vmem((poles, SUB, width), F32),
+            vmem((rows, width), BF16),
             dma((len(operands) + 2,)),
             dma((chunks,)),
             dma((chunks,)),
-            dma((2, rounds + 1)),
-            dma((2, rounds + 1)),
+            dma((2, slots)),
+            dma((2, slots)),
             dma((n_chan - 1,)),
             dma((n_chan - 1,)),
+            dma((2,)),
         ],
         compiler_params=pltpu.CompilerParams(
-            collective_id=0, has_side_effects=True, vmem_limit_bytes=40 * 1024 * 1024
+            collective_id=0, has_side_effects=True, vmem_limit_bytes=56 * 1024 * 1024
         ),
         cost_estimate=pl.CostEstimate(flops=int(8e9), bytes_accessed=int(8e6), transcendentals=0),
         name="filters",

time: 51 us -> 38.6 us (0.76)
  local copies, waits for them, and re-layouts: 11.2 us -> 0.01 us
  Pallas kernels: 37.7 us -> 35.1 us
  other arithmetic: 1.48 us -> 3.29 us
    unnamed x24 -> x4, local copies, waits for them, and re-layouts: 11.2 us -> 0.01 us
    pallas_call x1, Pallas kernels: 37.7 us -> 35.1 us  [on_device(): pl.pallas_call(functools.partial(fused_kernel, n_ctx, n_chan, chunk), in_...]
    convert_element_type x1, other arithmetic: 1.47 us -> 2.58 us  [on_device(): return (gated * scale[:, None] * norm_gain[None, :]).astype(BF16)]
    rsqrt x1, other arithmetic: 0.01 us -> 0.7 us  [on_device(): scale = lax.rsqrt(power[0] / channels + 1e-06)]
where the time goes in v2:
time: 38.6 us; the launch traced here: 38.4 us
  Pallas kernels  35.1 us (91%)
  other arithmetic  3.29 us (9%)
    pallas_call x1, Pallas kernels, on_device(): pl.pallas_call(functools.partial(fused_kernel, n_ctx, n_chan, chunk), in_...  35.1 us
    convert_element_type x1, other arithmetic, on_device(): return (gated * scale[:, None] * norm_gain[None, :]).astype(BF16)  2.58 us

profile of v2, /device:TPU:0, one launch (start us, length us, event | category | flops | bytes accessed | tf_op | source)
XLA Modules:
  0.0 38.4 jit_solution(3617821682755058304)
XLA Ops:
  0.0 0.0 copy-start
  0.0 0.0 copy-start.1
  0.0 35.1 %filters.1 = (bf16[256,2048]{1,0:T(8,128)(2,1)}, f32[8,256]{1,0:T(8,128)}) custom-call(bf16[256,2048]{1,0:T(8,128)(2,1)} %refs_0_.1, bf16[256,2048]{1,0:T(8,128)(2,1)} %refs_1_.1, bf16[256,2048]{1,0:T(8,128)(2,1)} %refs_2_.1, bf16[256,2048]{1,0:T(8,128)(2,1)} %refs_3_.1, f32[128,2048]{1,0:T(8,128)} %refs_4_.1, f32[16,2048]{1,0:T(8,128)} %refs_5_.1, ...), custom_call_target="tpu_custom_call" | custom-call | flops 8000000000 | bytes 8000000 | tf_op jit(solution)/shard_map/filters/pallas_call | solution.py:361
  35.1 0.7 %add_rsqrt_fusion = f32[1,256]{1,0:T(1,128)S(1)} fusion(f32[8,256]{1,0:T(8,128)} %get-tuple-element.8), kind=kLoop, calls=%fused_computation.1 | loop fusion | flops 512 | bytes 2048 | tf_op jit(solution)/shard_map/rsqrt | solution.py:401
  35.8 0.0 copy-done
  35.8 0.0 copy-done.1
  35.8 2.6 %multiply_convert_fusion = bf16[256,2048]{1,0:T(8,128)(2,1)} fusion(bf16[256,2048]{1,0:T(8,128)(2,1)} %get-tuple-element.7, bf16[256,2048]{1,0:T(8,128)(2,1)S(1)} %copy-done, f32[2048]{0:T(1024)S(1)} %copy-done.1, f32[256]{0:T(256)S(1)} %bitcast.2), kind=kLoop, calls=%fused_computation | loop fusion | flops 3145728 | bytes 3154944 | tf_op jit(solution)/shard_map/convert_element_type | solution.py:403
Async XLA Ops:
  0.0 35.8 %copy-start = (bf16[256,2048]{1,0:T(8,128)(2,1)S(1)}, bf16[256,2048]{1,0:T(8,128)(2,1)}, u32[]{:S(2)}) copy-start(bf16[256,2048]{1,0:T(8,128)(2,1)} %refs_3_.1) | copy-start | bytes 3145732
  0.0 35.8 %copy-start.1 = (f32[2048]{0:T(1024)S(1)}, f32[2048]{0:T(1024)}, u32[]{:S(2)}) copy-start(f32[2048]{0:T(1024)} %param.20) | copy-start | bytes 24580
